TPU v7x, 768 devices: a whole 4x8x12 slice. The times are simulated.
768 devices in a mesh: dp: 24 (over z, core), tensor: 32 (over x, y).
Axes of the slice: x: 4, y: 8, z: 12, core: 2. Of those that a mesh axis runs over, the one named last changes fastest.
Arguments:
- gradient: bfloat16 [576, 512, 512], P('dp', 'tensor'), may hold values from -16000 to 16000
- momentum: float32 [576, 512, 512], P('dp', 'tensor'), may hold values from -4 to 4
- eig_left: bfloat16 [1536, 512, 512], P(('dp', 'tensor')), may hold values from -0.25 to 0.25
- eig_right: bfloat16 [1536, 512, 512], P(('dp', 'tensor')), may hold values from -0.25 to 0.25
- row_stats: float32 [1536, 512], P(('dp', 'tensor')), may hold values from 0.01 to 0.2
- col_stats: float32 [1536, 512], P(('dp', 'tensor')), may hold values from 0.01 to 0.2
- owners: int32 [576, 1], P('dp'), may hold values from 0 to 31; in each aligned block of 24 rows (0 to 23, 24 to 47, ...) at most 2 rows name the same one
Outputs:
- new_momentum: float32 [576, 512, 512], P('dp', 'tensor')
- update: bfloat16 [576, 512, 512], P('dp', 'tensor')
- new_rows: float32 [1536, 512], P(('dp', 'tensor'))
- new_cols: float32 [1536, 512], P(('dp', 'tensor'))
Inputs may be any that keep to these rules, and one draw needn't show every extreme that they name: `owners`: among the 24 blocks of one data group no tensor index owns more than 2, and some index owns exactly 2.
All inputs are finite; a program needn't handle non-finite values.
Results may differ from a plain program's by a relative error of at most 0.0061.
Values may be sent and summed in bfloat16 or wider, within the bound.
A program may use at most 32 MiB of HBM per device.

v0:
```python
import math

import jax
import jax.numpy as jnp
from jax import lax
from jax.sharding import PartitionSpec as P

momentum_decay = 0.9
second_decay = 0.95
epsilon = 1e-08
clip_share = 0.25


def precondition(arrived, left_basis, right_basis, row_stats, col_stats, in_use):
    halves = jnp.einsum(
        "kij,kcil->kcjl", left_basis, arrived, preferred_element_type=jnp.float32
    ).astype(jnp.bfloat16)
    rotated = jnp.einsum("kcjl,klm->kcjm", halves, right_basis, preferred_element_type=jnp.float32)
    rot_grad = rotated[:, 0]
    rot_moment = rotated[:, 1]
    squares = rot_grad * rot_grad
    rows_next = second_decay * row_stats + (1.0 - second_decay) * jnp.mean(squares, axis=2)
    cols_next = second_decay * col_stats + (1.0 - second_decay) * jnp.mean(squares, axis=1)
    scale_hat = (
        rows_next[:, :, None] * cols_next[:, None, :] / jnp.mean(rows_next, axis=1)[:, None, None]
    )
    direction = (rot_moment / (jnp.sqrt(scale_hat) + epsilon)).astype(jnp.bfloat16)
    half_back = jnp.einsum(
        "kij,kjl->kil", left_basis, direction, preferred_element_type=jnp.float32
    ).astype(jnp.bfloat16)
    finished = jnp.einsum(
        "kil,kml->kim", half_back, right_basis, preferred_element_type=jnp.float32
    ).astype(jnp.bfloat16)
    kept_rows = jnp.where(in_use[:, None], rows_next, row_stats)
    kept_cols = jnp.where(in_use[:, None], cols_next, col_stats)
    return (finished, kept_rows, kept_cols)


def local(gradient, momentum, eig_left, eig_right, row_stats, col_stats, owners):
    group_blocks, strip_rows, block_size = gradient.shape
    owner_slots = eig_left.shape[0]
    tensor_size = lax.axis_size("tensor")
    whole_blocks = group_blocks * lax.axis_size("dp")
    widened = gradient.astype(jnp.float32)
    squared_sum = lax.psum(jnp.sum(widened * widened), ("dp", "tensor"))
    factor = jnp.minimum(
        1.0, clip_share * block_size * math.sqrt(whole_blocks) / jnp.sqrt(squared_sum)
    )
    clipped = widened * factor
    new_momentum = momentum_decay * momentum + (1.0 - momentum_decay) * clipped
    payload = jnp.stack([clipped.astype(jnp.bfloat16), new_momentum.astype(jnp.bfloat16)], axis=1)
    payload = payload.reshape(group_blocks, 2, strip_rows * block_size)
    holders = owners[:, 0]
    counter = jnp.arange(group_blocks, dtype=jnp.int32)
    same_owner = holders[:, None] == holders[None, :]
    before = counter[None, :] < counter[:, None]
    earlier_count = jnp.sum((same_owner & before).astype(jnp.int32), axis=1)
    slot_match = (
        earlier_count[None, None, :] == jnp.arange(owner_slots, dtype=jnp.int32)[:, None, None]
    )
    owner_match = holders[None, None, :] == jnp.arange(tensor_size, dtype=jnp.int32)[None, :, None]
    selector = (slot_match & owner_match).astype(jnp.bfloat16)
    outgoing = jnp.einsum(
        "kpb,bcx->kcpx", selector, payload, preferred_element_type=jnp.float32
    ).astype(jnp.bfloat16)
    owned_count = jnp.sum((holders == lax.axis_index("tensor")).astype(jnp.int32))
    in_use = jnp.arange(owner_slots, dtype=jnp.int32) < owned_count
    arrived = lax.all_to_all(outgoing, "tensor", split_axis=2, concat_axis=2, tiled=True)
    arrived = arrived.reshape(owner_slots, 2, block_size, block_size)
    finished, new_rows, new_cols = precondition(
        arrived, eig_left, eig_right, row_stats, col_stats, in_use
    )
    returned = lax.all_to_all(
        finished.reshape(owner_slots, tensor_size, strip_rows * block_size),
        "tensor",
        split_axis=1,
        concat_axis=1,
        tiled=True,
    )
    update = jnp.einsum(
        "kpb,kpx->bx", selector, returned, preferred_element_type=jnp.float32
    ).astype(jnp.bfloat16)
    update = update.reshape(group_blocks, strip_rows, block_size)
    return (new_momentum, update, new_rows, new_cols)


def solution(mesh):
    placed = (
        P("dp", "tensor", None),
        P("dp", "tensor", None),
        P(("dp", "tensor"), None, None),
        P(("dp", "tensor"), None, None),
        P(("dp", "tensor"), None),
        P(("dp", "tensor"), None),
        P("dp", None),
    )
    return jax.shard_map(
        local,
        mesh=mesh,
        in_specs=placed,
        out_specs=(
            P("dp", "tensor", None),
            P("dp", "tensor", None),
            P(("dp", "tensor"), None),
            P(("dp", "tensor"), None),
        ),
        check_vma=False,
    )
```

profile of v0, /device:TPU:8, one launch (start us, length us, event | category | flops | bytes accessed | tf_op | source)
XLA Modules:
  0.0 242.9 jit_solution(10444286996061015298)
XLA Ops:
  0.6 0.0 copy-start
  0.6 1.9 fusion.26
  2.5 0.7 iota_compare_fusion
  3.3 0.9 convert_reduce_fusion
  4.2 116.6 %psum.7 = f32[]{:T(128)} all-reduce(f32[]{:T(128)} %fusion.26), channel_id=1, replica_groups=mesh['dp'=24,'tensor'=32] {'dp','tensor'}, use_global_device_ids=true, to_apply=%region_1.0 | all-reduce | flops 1 | bytes 8 | tf_op jit(solution)/shard_map/psum | solution.py:45
  121.5 2.4 fusion.39
  123.9 0.2 stack.10
  124.0 0.2 stack.9
  124.2 0.8 fusion
  125.1 3.5 %copy.22 = bf16[2,2,32,8192]{3,0,1,2:T(2,128)(2,1)} copy(bf16[2,2,32,8192]{3,2,0,1:T(8,128)(2,1)S(1)} %fusion) | data formatting | bytes 4194304 | tf_op jit(solution)/shard_map/convert_element_type | solution.py:65
  128.6 0.0 copy-start.3
  128.6 9.1 %all-to-all-start = ((bf16[2,2,32,8192]{3,0,1,2:T(2,128)(2,1)}), bf16[2,2,32,8192]{3,0,1,2:T(2,128)(2,1)S(1)}, u32[]{:S(2)}, u32[]{:S(2)}) async-start(bf16[2,2,32,8192]{3,0,1,2:T(2,128)(2,1)} %copy.22), calls=%async_computation | async-start | bytes 4194304 | tf_op jit(solution)/shard_map/all_to_all | solution.py:68
  137.8 0.0 copy-done.3
  137.8 0.6 fusion.35
  138.4 0.6 iota_compare_fusion.3
  139.1 47.7 %all-to-all-done = bf16[2,2,32,8192]{3,0,1,2:T(2,128)(2,1)S(1)} async-done(((bf16[2,2,32,8192]{3,0,1,2:T(2,128)(2,1)}), bf16[2,2,32,8192]{3,0,1,2:T(2,128)(2,1)S(1)}, u32[]{:S(2)}, u32[]{:S(2)}) %all-to-all-start) | async-done | bytes 2097184 | tf_op jit(solution)/shard_map/all_to_all | solution.py:68
  186.8 2.5 %copy.23 = bf16[2,2,32,8192]{3,2,1,0:T(8,128)(2,1)} copy(bf16[2,2,32,8192]{3,0,1,2:T(2,128)(2,1)S(1)} %all-to-all-done) | data formatting | bytes 4194304 | tf_op jit(solution)/shard_map/all_to_all | solution.py:68
  189.3 2.9 %reshape.82 = bf16[2,2,512,512]{3,2,1,0:T(8,128)(2,1)S(1)} reshape(bf16[2,2,32,8192]{3,2,1,0:T(8,128)(2,1)} %copy.23) | data formatting | bytes 4194304 | tf_op jit(solution)/shard_map/reshape | solution.py:69
  192.2 0.0 copy-done
  192.2 5.5 %fusion.4 = f32[2,2,512,512]{3,2,1,0:T(8,128)} fusion(bf16[2,2,512,512]{3,2,1,0:T(8,128)(2,1)S(1)} %reshape.82, bf16[2,512,512]{2,1,0:T(8,128)(2,1)S(1)} %copy-done, bf16[2,512,512]{2,1,0:T(8,128)(2,1)} %param.9), kind=kOutput, calls=%fused_computation.8 | convolution fusion | flops 2148532224 | bytes 8388608 | tf_op jit(solution)/shard_map/kcjl,klm->kcjm/dot_general | solution.py:18
  197.8 0.0 copy-start.1
  197.8 0.0 copy-start.2
  197.8 1.9 fusion.7
  199.7 0.0 copy-done.1
  199.7 0.0 copy-done.2
  199.7 0.7 broadcast_select_fusion
  200.4 0.1 reduce_sum.58
  200.5 4.0 %convolution_convert_fusion.1 = bf16[2,512,512]{2,1,0:T(8,128)(2,1)S(1)} fusion(bf16[2,512,512]{2,1,0:T(8,128)(2,1)S(1)} %copy-done, bf16[2,512,512]{2,1,0:T(8,128)(2,1)} %param.9, f32[2,2,512,512]{3,2,1,0:T(8,128)} %fusion.4, f32[2]{0:T(128)S(1)} %broadcast_multiply_fusion, f32[2,512]{1,0:T(2,128)S(1)} %get-tuple-element.12, ...), kind=kOutput, calls=%fused_computation.14 | convolution fusion | flops 1077411840 | bytes 5251080 | tf_op jit(solution)/shard_map/kil,kml->kim/dot_general | solution.py:31
  204.5 0.5 reshape.83
  205.0 1.1 copy.28
  206.1 35.2 %all_to_all.10 = bf16[2,32,8192]{2,0,1:T(2,128)(2,1)S(1)} all-to-all(bf16[2,32,8192]{2,0,1:T(2,128)(2,1)S(1)} %copy.28), channel_id=1, replica_groups=mesh['dp'=24,'tensor'=32] {'tensor'}, dimensions={1} | all-to-all | bytes 2097152 | tf_op jit(solution)/shard_map/all_to_all | solution.py:73
  241.3 0.7 fusion.1
  242.0 0.9 copy.37
  (2 shorter events, 0.0 us)
Async XLA Ops:
  0.6 191.6 %copy-start = (bf16[2,512,512]{2,1,0:T(8,128)(2,1)S(1)}, bf16[2,512,512]{2,1,0:T(8,128)(2,1)}, u32[]{:S(2)}) copy-start(bf16[2,512,512]{2,1,0:T(8,128)(2,1)} %param.10) | copy-start | bytes 3145732
  128.6 9.2 %copy-start.3 = (s32[24,1]{0,1:T(1,128)S(1)}, s32[24,1]{0,1:T(1,128)}, u32[]{:S(2)}) copy-start(s32[24,1]{0,1:T(1,128)} %param.13) | copy-start | bytes 292
  128.6 58.2 %all-to-all-start = ((bf16[2,2,32,8192]{3,0,1,2:T(2,128)(2,1)}), bf16[2,2,32,8192]{3,0,1,2:T(2,128)(2,1)S(1)}, u32[]{:S(2)}, u32[]{:S(2)}) async-start(bf16[2,2,32,8192]{3,0,1,2:T(2,128)(2,1)} %copy.22), calls=%async_computation | async-start | bytes 4194304 | tf_op jit(solution)/shard_map/all_to_all | solution.py:68
  197.8 1.9 copy-start.1
  197.8 1.9 copy-start.2
where the time goes:
time: 243 us
  blocking collectives  152 us (63%)
  waiting for transfers between devices  47.7 us (20%)
  local copies, waits for them, and re-layouts  11.8 us (5%)
  matrix products  11.1 us (5%)
  other arithmetic  9.89 us (4%)
  starting transfers between devices  9.14 us (4%)
    psum x1, blocking collectives, local(): squared_sum = lax.psum(jnp.sum(widened * widened), ('dp', 'tensor'))  117 us
    all_to_all x1, waiting for transfers between devices, local(): lax.all_to_all(outgoing, 'tensor', split_axis=2, concat_axis=2, tiled=True)  47.7 us
    all_to_all x1, blocking collectives, local(): lax.all_to_all(finished.reshape(owner_slots, tensor_size, strip_rows * bl...  35.2 us
    all_to_all x1, starting transfers between devices, local(): lax.all_to_all(outgoing, 'tensor', split_axis=2, concat_axis=2, tiled=True)  9.14 us
    dot_general x1, matrix products, precondition(): jnp.einsum('kcjl,klm->kcjm', halves, right_basis, preferred_element_type=...  5.55 us
  transfers between devices with their start and end apart: 1, of which 1 were waited for; matrix products, arithmetic and copies ran while one was open for 1% of the time, Pallas kernels for 0%

commit v1 on v0

v1 whole, which is shorter than its diff:
```python
import functools
import math

import jax
import jax.numpy as jnp
from jax import lax
from jax.experimental import pallas as pl
from jax.experimental.pallas import tpu as pltpu
from jax.sharding import PartitionSpec as P

momentum_decay = 0.9
second_decay = 0.95
epsilon = 1e-08
clip_share = 0.25
columns = 8
chunk = 128
MESH = pl.DeviceIdType.MESH
f32 = jnp.float32
bf16 = jnp.bfloat16


def dot(a, b):
    return jnp.dot(a, b, preferred_element_type=f32)


def to_column(row):
    return jnp.broadcast_to(row, (128, row.shape[1])).T[:, 0:1]


def to_row(column):
    return jnp.broadcast_to(column, (column.shape[0], 128)).T[0:1, :]


def kernel(
    n_dp,
    n_tensor,
    clip_norm,
    owners,
    gradient,
    momentum,
    left,
    right,
    row_stats,
    col_stats,
    new_momentum,
    update,
    new_rows,
    new_cols,
    grad_v,
    mom_v,
    moment_v,
    update_v,
    left_v,
    right_v,
    left_t,
    right_t,
    inverse,
    out_g,
    out_m,
    out_u,
    in_g,
    in_m,
    in_u,
    sums_t,
    sums_d,
    chosen_v,
    chosen,
    local_sem,
    send_sem,
    recv_sem,
):
    blocks, strip, size = grad_v.shape
    me = lax.axis_index("tensor")
    group = lax.axis_index("dp")
    my_x = me // columns
    my_y = lax.rem(me, columns)
    barrier = pltpu.get_barrier_semaphore()

    @pl.loop(1, n_tensor)
    def _(i):
        pl.semaphore_signal(
            barrier, inc=1, device_id={"tensor": lax.rem(me + i, n_tensor)}, device_id_type=MESH
        )

    @pl.loop(1, n_dp)
    def _(i):
        pl.semaphore_signal(
            barrier, inc=1, device_id={"dp": lax.rem(group + i, n_dp)}, device_id_type=MESH
        )

    load_g = pltpu.make_async_copy(gradient, grad_v, local_sem.at[0])
    load_m = pltpu.make_async_copy(momentum, mom_v, local_sem.at[1])
    load_l = pltpu.make_async_copy(left, left_v, local_sem.at[2])
    load_r = pltpu.make_async_copy(right, right_v, local_sem.at[3])
    load_g.start()
    load_m.start()
    load_l.start()
    load_r.start()

    lane = lax.broadcasted_iota(jnp.int32, (8, 128), 1)
    level = lax.broadcasted_iota(jnp.int32, (8, 128), 0)
    first = jnp.full((8, 128), -1, jnp.int32)
    second = first
    for b in range(blocks):
        mine = lane == owners[b, 0]
        second = jnp.where(mine & (first >= 0), b, second)
        first = jnp.where(mine & (first < 0), b, first)
    chosen_v[...] = jnp.where(level == 0, first, second)
    load_c = pltpu.make_async_copy(chosen_v, chosen, local_sem.at[4])
    load_c.start()
    load_g.wait()

    def squares(b, total):
        wide = grad_v[b].astype(f32)
        wide = wide * wide
        for j in range(size // 128):
            for i in range(strip // 8):
                total = total + wide[8 * i : 8 * i + 8, 128 * j : 128 * j + 128]
        return total

    sums_t[me] = lax.fori_loop(0, blocks, squares, jnp.zeros((8, 128), f32))
    load_c.wait()

    def pack(source, target):
        @pl.loop(0, n_tensor)
        def _(p):
            for k in range(2):
                target[k, p] = source[jnp.maximum(chosen[k, p], 0)]

    def strip_of(p):
        return pl.ds(pl.multiple_of(p * strip, strip), strip)

    def scatter(source, target, k, number):
        @pl.loop(1, n_tensor)
        def _(i):
            dx = i // columns
            j = lax.rem(i, columns)
            odd = lax.rem(j, 2)
            dy = odd * ((j + 1) // 2) + (1 - odd) * lax.rem(columns - j // 2, columns)
            p = lax.rem(my_x + dx, n_tensor // columns) * columns + lax.rem(my_y + dy, columns)
            pltpu.make_async_remote_copy(
                src_ref=source.at[k, p],
                dst_ref=target.at[k, strip_of(me)],
                send_sem=send_sem.at[number],
                recv_sem=recv_sem.at[number],
                device_id={"tensor": p},
                device_id_type=MESH,
            ).start()

    def waiter(ref, number):
        return pltpu.make_async_remote_copy(
            src_ref=ref,
            dst_ref=ref,
            send_sem=send_sem.at[number],
            recv_sem=recv_sem.at[number],
            device_id={"tensor": lax.rem(me + 1, n_tensor)},
            device_id_type=MESH,
        )

    others = pl.ds(0, (n_tensor - 1) * strip)
    pack(grad_v, out_g)
    pl.semaphore_wait(barrier, n_tensor + n_dp - 2)

    @pl.loop(1, n_tensor)
    def _(i):
        pltpu.make_async_remote_copy(
            src_ref=sums_t.at[me],
            dst_ref=sums_t.at[me],
            send_sem=send_sem.at[0],
            recv_sem=recv_sem.at[0],
            device_id={"tensor": lax.rem(me + i, n_tensor)},
            device_id_type=MESH,
        ).start()

    scatter(out_g, in_g, 0, 2)
    in_g[0, strip_of(me)] = out_g[0, me]
    in_g[1, strip_of(me)] = out_g[1, me]
    waiter(sums_t.at[pl.ds(0, n_tensor - 1)], 0).wait_recv()
    sums_d[group] = jnp.sum(sums_t[...], axis=0)

    @pl.loop(1, n_dp)
    def _(i):
        pltpu.make_async_remote_copy(
            src_ref=sums_d.at[group],
            dst_ref=sums_d.at[group],
            send_sem=send_sem.at[1],
            recv_sem=recv_sem.at[1],
            device_id={"dp": lax.rem(group + i, n_dp)},
            device_id_type=MESH,
        ).start()

    scatter(out_g, in_g, 1, 3)
    load_l.wait()
    load_r.wait()
    for k in range(2):
        left_t[k] = left_v[k].T
        right_t[k] = right_v[k].T
    load_m.wait()
    waiter(sums_d.at[pl.ds(0, n_dp - 1)], 1).wait_recv()
    squared_sum = jnp.sum(jnp.sum(sums_d[...], axis=0), keepdims=True)
    limit = clip_norm * clip_norm
    factor = jnp.where(
        squared_sum > limit, clip_norm / jnp.sqrt(jnp.maximum(squared_sum, limit)), 1.0
    )

    @pl.loop(0, blocks)
    def _(b):
        clipped = grad_v[b].astype(f32) * factor
        moved = momentum_decay * mom_v[b] + (1.0 - momentum_decay) * clipped
        mom_v[b] = moved
        moment_v[b] = moved.astype(bf16)

    store_m = pltpu.make_async_copy(mom_v, new_momentum, local_sem.at[1])
    store_m.start()
    pack(moment_v, out_m)
    for k in range(2):
        scatter(out_m, in_m, k, 4 + k)
        in_m[k, strip_of(me)] = out_m[k, me]

    share = factor * factor * ((1.0 - second_decay) / size)
    for k in range(2):
        waiter(in_g.at[k, others], 2 + k).wait_recv()
        half = dot(left_t[k], in_g[k]).astype(bf16)
        rotated = dot(half, right_v[k])
        square = rotated * rotated
        rows_old = row_stats[k : k + 1, :]
        cols_old = col_stats[k : k + 1, :]
        rows_next = second_decay * to_column(rows_old) + share * jnp.sum(
            square, axis=1, keepdims=True
        )
        cols_next = second_decay * cols_old + share * jnp.sum(square, axis=0, keepdims=True)
        mean = jnp.sum(rows_next, axis=0, keepdims=True) * (1.0 / size)
        inverse[k] = 1.0 / (jnp.sqrt(rows_next / mean) * jnp.sqrt(cols_next) + epsilon)
        used = jnp.full((1, size), chosen[k, me], jnp.int32) >= 0
        new_rows[k : k + 1, :] = jnp.where(used, to_row(rows_next), rows_old)
        new_cols[k : k + 1, :] = jnp.where(used, cols_next, cols_old)

    for k in range(2):
        waiter(in_m.at[k, others], 4 + k).wait_recv()
        half = dot(left_t[k], in_m[k]).astype(bf16)
        direction = (dot(half, right_v[k]) * inverse[k]).astype(bf16)
        for j in range(n_tensor // columns):
            c = lax.rem(my_x + j, n_tensor // columns)
            band = pl.ds(pl.multiple_of(c * chunk, chunk), chunk)
            half_back = dot(left_v[k, band], direction).astype(bf16)
            out_u[k, band] = dot(half_back, right_t[k]).astype(bf16)

            @pl.loop(1 if j == 0 else 0, columns)
            def _(i):
                p = c * columns + lax.rem(my_y + i, columns)
                pltpu.make_async_remote_copy(
                    src_ref=out_u.at[k, strip_of(p)],
                    dst_ref=in_u.at[k, me],
                    send_sem=send_sem.at[6 + k],
                    recv_sem=recv_sem.at[6 + k],
                    device_id={"tensor": p},
                    device_id_type=MESH,
                ).start()

        in_u[k, me] = out_u[k, strip_of(me)]

    for k in range(2):
        waiter(in_u.at[k, pl.ds(0, n_tensor - 1)], 6 + k).wait_recv()

    @pl.loop(0, blocks)
    def _(b):
        o = owners[b, 0]
        rank = (chosen[0, o] != b).astype(jnp.int32)
        update_v[b] = in_u[rank, o]

    store_u = pltpu.make_async_copy(update_v, update, local_sem.at[0])
    store_u.start()
    waiter(sums_t.at[pl.ds(0, n_tensor - 1)], 0).wait_send()
    waiter(sums_d.at[pl.ds(0, n_dp - 1)], 1).wait_send()
    for k in range(2):
        waiter(in_g.at[k, others], 2 + k).wait_send()
        waiter(in_m.at[k, others], 4 + k).wait_send()
        waiter(in_u.at[k, pl.ds(0, n_tensor - 1)], 6 + k).wait_send()
    store_m.wait()
    store_u.wait()


def local(n_dp, n_tensor, gradient, momentum, eig_left, eig_right, row_stats, col_stats, owners):
    blocks, strip, size = gradient.shape
    slots = eig_left.shape[0]
    clip_norm = clip_share * size * math.sqrt(blocks * n_dp)
    anywhere = pl.BlockSpec(memory_space=pl.ANY)
    vmem = pl.BlockSpec(memory_space=pltpu.VMEM)
    square = (slots, size, size)
    pieces = (slots, n_tensor, strip, size)
    return pl.pallas_call(
        functools.partial(kernel, n_dp, n_tensor, clip_norm),
        out_shape=(
            jax.ShapeDtypeStruct(momentum.shape, f32),
            jax.ShapeDtypeStruct(gradient.shape, bf16),
            jax.ShapeDtypeStruct(row_stats.shape, f32),
            jax.ShapeDtypeStruct(col_stats.shape, f32),
        ),
        in_specs=[
            pl.BlockSpec(memory_space=pltpu.SMEM),
            anywhere,
            anywhere,
            anywhere,
            anywhere,
            vmem,
            vmem,
        ],
        out_specs=(anywhere, anywhere, vmem, vmem),
        scratch_shapes=[
            pltpu.VMEM(gradient.shape, bf16),
            pltpu.VMEM(gradient.shape, f32),
            pltpu.VMEM(gradient.shape, bf16),
            pltpu.VMEM(gradient.shape, bf16),
            pltpu.VMEM(square, bf16),
            pltpu.VMEM(square, bf16),
            pltpu.VMEM(square, bf16),
            pltpu.VMEM(square, bf16),
            pltpu.VMEM(square, f32),
            pltpu.VMEM(pieces, bf16),
            pltpu.VMEM(pieces, bf16),
            pltpu.VMEM(square, bf16),
            pltpu.VMEM(square, bf16),
            pltpu.VMEM(square, bf16),
            pltpu.VMEM(pieces, bf16),
            pltpu.VMEM((n_tensor, 8, 128), f32),
            pltpu.VMEM((n_dp, 8, 128), f32),
            pltpu.VMEM((8, 128), jnp.int32),
            pltpu.SMEM((8, 128), jnp.int32),
            pltpu.SemaphoreType.DMA((5,)),
            pltpu.SemaphoreType.DMA((8,)),
            pltpu.SemaphoreType.DMA((8,)),
        ],
        compiler_params=pltpu.CompilerParams(
            collective_id=0, has_side_effects=True, vmem_limit_bytes=48 << 20
        ),
        name="soap_step",
    )(owners, gradient, momentum, eig_left, eig_right, row_stats, col_stats)


def solution(mesh):
    placed = (
        P("dp", "tensor", None),
        P("dp", "tensor", None),
        P(("dp", "tensor"), None, None),
        P(("dp", "tensor"), None, None),
        P(("dp", "tensor"), None),
        P(("dp", "tensor"), None),
        P("dp", None),
    )
    return jax.shard_map(
        functools.partial(local, mesh.shape["dp"], mesh.shape["tensor"]),
        mesh=mesh,
        in_specs=placed,
        out_specs=(
            P("dp", "tensor", None),
            P("dp", "tensor", None),
            P(("dp", "tensor"), None),
            P(("dp", "tensor"), None),
        ),
        check_vma=False,
    )
```

time: 243 us -> 104 us (0.43)
  the two profiles are of different devices: /device:TPU:8 before, /device:TPU:2 now
where the time goes in v1:
time: 104 us; the launch traced here: 103 us
  Pallas kernels  94.6 us (91%)
  local copies, waits for them, and re-layouts  8.14 us (8%)
    pallas_call x1, Pallas kernels, local(): pl.pallas_call(functools.partial(kernel, n_dp, n_tensor, clip_norm), out_...  94.6 us
    unnamed x17, local copies, waits for them, and re-layouts  8.14 us

profile of v1, /device:TPU:2, one launch (start us, length us, event | category | flops | bytes accessed | tf_op | source)
XLA Modules:
  0.0 103.4 jit_solution(14534247340119776742)
XLA Ops:
  0.6 0.0 copy-start.5
  0.6 0.0 copy-start.4
  0.7 0.7 copy.11.owners
  1.4 0.0 copy-done.5
  1.4 0.0 copy-done.4
  1.4 0.0 copy-start
  1.4 1.2 %copy-done = bf16[2,512,512]{2,1,0:T(8,128)(2,1)S(1)} copy-done((bf16[2,512,512]{2,1,0:T(8,128)(2,1)S(1)}, bf16[2,512,512]{2,1,0:T(8,128)(2,1)}, u32[]{:S(2)}) %copy-start) | copy-done | bytes 1048600
  2.6 0.0 copy-start.1
  2.6 1.2 %copy-done.1 = bf16[2,512,512]{2,1,0:T(8,128)(2,1)S(1)} copy-done((bf16[2,512,512]{2,1,0:T(8,128)(2,1)S(1)}, bf16[2,512,512]{2,1,0:T(8,128)(2,1)}, u32[]{:S(2)}) %copy-start.1) | copy-done | bytes 1048600
  3.9 0.0 copy-start.2
  3.9 1.1 %copy-done.2 = f32[24,16,512]{2,1,0:T(8,128)S(1)} copy-done((f32[24,16,512]{2,1,0:T(8,128)S(1)}, f32[24,16,512]{2,1,0:T(8,128)}, u32[]{:S(2)}) %copy-start.2) | copy-done | bytes 786456
  5.0 0.0 copy-start.3
  5.0 1.0 copy-done.3
  6.0 94.6 %soap_step.1 = (f32[24,16,512]{2,1,0:T(8,128)S(1)}, bf16[24,16,512]{2,1,0:T(8,128)(2,1)S(1)}, f32[2,512]{1,0:T(2,128)S(1)}, f32[2,512]{1,0:T(2,128)S(1)}) custom-call(s32[24,1]{1,0:T(8,128)S(1)} %copy.11.owners, bf16[24,16,512]{2,1,0:T(8,128)(2,1)S(1)} %copy-done.3, f32[24,16,512]{2,1,0:T(8,128)S(1)} %copy-done.2, bf16[2,512,512]{2,1,0:T(8,128)(2,1)S(1)} %copy-done, ...), custom_call_target="tpu_custom_call" | custom-call | tf_op jit(solution)/shard_map/soap_step/pallas_call | solution.py:291
  100.6 0.9 copy.16
  101.4 0.7 copy.17
  102.2 0.6 copy.18
  102.8 0.6 copy.19
Async XLA Ops:
  0.6 0.8 copy-start.5
  0.6 0.8 copy-start.4
  1.4 1.2 %copy-start = (bf16[2,512,512]{2,1,0:T(8,128)(2,1)S(1)}, bf16[2,512,512]{2,1,0:T(8,128)(2,1)}, u32[]{:S(2)}) copy-start(bf16[2,512,512]{2,1,0:T(8,128)(2,1)} %left.1) | copy-start | bytes 3145732
  2.6 1.2 %copy-start.1 = (bf16[2,512,512]{2,1,0:T(8,128)(2,1)S(1)}, bf16[2,512,512]{2,1,0:T(8,128)(2,1)}, u32[]{:S(2)}) copy-start(bf16[2,512,512]{2,1,0:T(8,128)(2,1)} %right.1) | copy-start | bytes 3145732
  3.9 1.1 %copy-start.2 = (f32[24,16,512]{2,1,0:T(8,128)S(1)}, f32[24,16,512]{2,1,0:T(8,128)}, u32[]{:S(2)}) copy-start(f32[24,16,512]{2,1,0:T(8,128)} %momentum.1) | copy-start | bytes 2359300
  5.0 1.0 copy-start.3

commit v2 on v1

--- a/solution.py
+++ b/solution.py
@@ -13,6 +13,7 @@
 epsilon = 1e-08
 clip_share = 0.25
 columns = 8
+lead = 11
 chunk = 128
 MESH = pl.DeviceIdType.MESH
 f32 = jnp.float32
@@ -63,6 +64,7 @@
     in_u,
     sums_t,
     sums_d,
+    total,
     chosen_v,
     chosen,
     local_sem,
@@ -82,11 +84,13 @@
             barrier, inc=1, device_id={"tensor": lax.rem(me + i, n_tensor)}, device_id_type=MESH
         )
 
-    @pl.loop(1, n_dp)
-    def _(i):
-        pl.semaphore_signal(
-            barrier, inc=1, device_id={"dp": lax.rem(group + i, n_dp)}, device_id_type=MESH
-        )
+    @pl.when(me == lead)
+    def _():
+        @pl.loop(1, n_dp)
+        def _(i):
+            pl.semaphore_signal(
+                barrier, inc=1, device_id={"dp": lax.rem(group + i, n_dp)}, device_id_type=MESH
+            )
 
     load_g = pltpu.make_async_copy(gradient, grad_v, local_sem.at[0])
     load_m = pltpu.make_async_copy(momentum, mom_v, local_sem.at[1])
@@ -102,7 +106,7 @@
     first = jnp.full((8, 128), -1, jnp.int32)
     second = first
     for b in range(blocks):
-        mine = lane == owners[b, 0]
+        mine = lane == owners[0, b]
         second = jnp.where(mine & (first >= 0), b, second)
         first = jnp.where(mine & (first < 0), b, first)
     chosen_v[...] = jnp.where(level == 0, first, second)
@@ -118,14 +122,13 @@
                 total = total + wide[8 * i : 8 * i + 8, 128 * j : 128 * j + 128]
         return total
 
-    sums_t[me] = lax.fori_loop(0, blocks, squares, jnp.zeros((8, 128), f32))
-    load_c.wait()
-
-    def pack(source, target):
-        @pl.loop(0, n_tensor)
+    mine = lax.fori_loop(0, blocks, squares, jnp.zeros((8, 128), f32))
+    sums_t[me] = jnp.sum(mine, axis=0, keepdims=True)
+
+    def pack(source, target, k):
+        @pl.loop(0, n_tensor, unroll=4)
         def _(p):
-            for k in range(2):
-                target[k, p] = source[jnp.maximum(chosen[k, p], 0)]
+            target[k, p] = source[jnp.maximum(chosen[k, p], 0)]
 
     def strip_of(p):
         return pl.ds(pl.multiple_of(p * strip, strip), strip)
@@ -158,46 +161,60 @@
         )
 
     others = pl.ds(0, (n_tensor - 1) * strip)
-    pack(grad_v, out_g)
-    pl.semaphore_wait(barrier, n_tensor + n_dp - 2)
-
-    @pl.loop(1, n_tensor)
-    def _(i):
+
+    def send_sum(source, target, number, peer):
         pltpu.make_async_remote_copy(
-            src_ref=sums_t.at[me],
-            dst_ref=sums_t.at[me],
-            send_sem=send_sem.at[0],
-            recv_sem=recv_sem.at[0],
-            device_id={"tensor": lax.rem(me + i, n_tensor)},
+            src_ref=source,
+            dst_ref=target,
+            send_sem=send_sem.at[number],
+            recv_sem=recv_sem.at[number],
+            device_id=peer,
             device_id_type=MESH,
         ).start()
 
-    scatter(out_g, in_g, 0, 2)
-    in_g[0, strip_of(me)] = out_g[0, me]
-    in_g[1, strip_of(me)] = out_g[1, me]
-    waiter(sums_t.at[pl.ds(0, n_tensor - 1)], 0).wait_recv()
-    sums_d[group] = jnp.sum(sums_t[...], axis=0)
-
-    @pl.loop(1, n_dp)
-    def _(i):
-        pltpu.make_async_remote_copy(
-            src_ref=sums_d.at[group],
-            dst_ref=sums_d.at[group],
-            send_sem=send_sem.at[1],
-            recv_sem=recv_sem.at[1],
-            device_id={"dp": lax.rem(group + i, n_dp)},
-            device_id_type=MESH,
-        ).start()
-
-    scatter(out_g, in_g, 1, 3)
+    sum_of_t = sums_t.at[pl.ds(0, n_tensor - 1)]
+    sum_of_d = sums_d.at[pl.ds(0, n_dp - 1)]
+
+    @pl.when(me == lead)
+    def _():
+        pl.semaphore_wait(barrier, n_tensor + n_dp - 2)
+        waiter(sum_of_t, 0).wait_recv()
+        sums_d[group] = jnp.sum(sums_t[...], axis=0)
+
+        @pl.loop(1, n_dp)
+        def _(i):
+            peer = {"dp": lax.rem(group + i, n_dp)}
+            send_sum(sums_d.at[group], sums_d.at[group], 1, peer)
+
+        waiter(sum_of_d, 1).wait_recv()
+        total[...] = jnp.sum(sums_d[...], axis=0)
+
+        @pl.loop(1, n_tensor)
+        def _(i):
+            send_sum(total, total, 8, {"tensor": lax.rem(lead + i, n_tensor)})
+
+    @pl.when(me != lead)
+    def _():
+        pl.semaphore_wait(barrier, n_tensor - 1)
+        send_sum(sums_t.at[me], sums_t.at[me], 0, {"tensor": lead})
+
+    load_c.wait()
+    for k in range(2):
+        pack(grad_v, out_g, k)
+        scatter(out_g, in_g, k, 2 + k)
+        in_g[k, strip_of(me)] = out_g[k, me]
     load_l.wait()
     load_r.wait()
     for k in range(2):
         left_t[k] = left_v[k].T
         right_t[k] = right_v[k].T
     load_m.wait()
-    waiter(sums_d.at[pl.ds(0, n_dp - 1)], 1).wait_recv()
-    squared_sum = jnp.sum(jnp.sum(sums_d[...], axis=0), keepdims=True)
+
+    @pl.when(me != lead)
+    def _():
+        waiter(total, 8).wait_recv()
+
+    squared_sum = jnp.sum(total[...], keepdims=True)
     limit = clip_norm * clip_norm
     factor = jnp.where(
         squared_sum > limit, clip_norm / jnp.sqrt(jnp.maximum(squared_sum, limit)), 1.0
@@ -212,8 +229,8 @@
 
     store_m = pltpu.make_async_copy(mom_v, new_momentum, local_sem.at[1])
     store_m.start()
-    pack(moment_v, out_m)
-    for k in range(2):
+    for k in range(2):
+        pack(moment_v, out_m, k)
         scatter(out_m, in_m, k, 4 + k)
         in_m[k, strip_of(me)] = out_m[k, me]
 
@@ -264,14 +281,22 @@
 
     @pl.loop(0, blocks)
     def _(b):
-        o = owners[b, 0]
+        o = owners[0, b]
         rank = (chosen[0, o] != b).astype(jnp.int32)
         update_v[b] = in_u[rank, o]
 
     store_u = pltpu.make_async_copy(update_v, update, local_sem.at[0])
     store_u.start()
-    waiter(sums_t.at[pl.ds(0, n_tensor - 1)], 0).wait_send()
-    waiter(sums_d.at[pl.ds(0, n_dp - 1)], 1).wait_send()
+
+    @pl.when(me == lead)
+    def _():
+        waiter(sum_of_d, 1).wait_send()
+        waiter(sum_of_t, 8).wait_send()
+
+    @pl.when(me != lead)
+    def _():
+        waiter(total, 0).wait_send()
+
     for k in range(2):
         waiter(in_g.at[k, others], 2 + k).wait_send()
         waiter(in_m.at[k, others], 4 + k).wait_send()
@@ -280,28 +305,46 @@
     store_u.wait()
 
 
+def store(*refs):
+    copies = [
+        pltpu.make_async_copy(refs[i], refs[4 + i], refs[8].at[i]) for i in range(4)
+    ]
+    for copy in copies:
+        copy.start()
+    for copy in copies:
+        copy.wait()
+
+
+def in_hbm(x):
+    return pltpu.with_memory_space_constraint(x, pltpu.HBM)
+
+
 def local(n_dp, n_tensor, gradient, momentum, eig_left, eig_right, row_stats, col_stats, owners):
     blocks, strip, size = gradient.shape
     slots = eig_left.shape[0]
     clip_norm = clip_share * size * math.sqrt(blocks * n_dp)
     anywhere = pl.BlockSpec(memory_space=pl.ANY)
+    hbm = pl.BlockSpec(memory_space=pltpu.HBM)
     vmem = pl.BlockSpec(memory_space=pltpu.VMEM)
     square = (slots, size, size)
     pieces = (slots, n_tensor, strip, size)
-    return pl.pallas_call(
+    shapes = (
+        jax.ShapeDtypeStruct(momentum.shape, f32),
+        jax.ShapeDtypeStruct(gradient.shape, bf16),
+        jax.ShapeDtypeStruct(row_stats.shape, f32),
+        jax.ShapeDtypeStruct(col_stats.shape, f32),
+    )
+    arguments = (owners.reshape(1, blocks), gradient, momentum)
+    arguments += (eig_left, eig_right, row_stats, col_stats)
+    results = pl.pallas_call(
         functools.partial(kernel, n_dp, n_tensor, clip_norm),
-        out_shape=(
-            jax.ShapeDtypeStruct(momentum.shape, f32),
-            jax.ShapeDtypeStruct(gradient.shape, bf16),
-            jax.ShapeDtypeStruct(row_stats.shape, f32),
-            jax.ShapeDtypeStruct(col_stats.shape, f32),
-        ),
+        out_shape=shapes,
         in_specs=[
             pl.BlockSpec(memory_space=pltpu.SMEM),
-            anywhere,
-            anywhere,
-            anywhere,
-            anywhere,
+            hbm,
+            hbm,
+            hbm,
+            hbm,
             vmem,
             vmem,
         ],
@@ -322,19 +365,29 @@
             pltpu.VMEM(square, bf16),
             pltpu.VMEM(square, bf16),
             pltpu.VMEM(pieces, bf16),
-            pltpu.VMEM((n_tensor, 8, 128), f32),
-            pltpu.VMEM((n_dp, 8, 128), f32),
+            pltpu.VMEM((n_tensor, 1, 128), f32),
+            pltpu.VMEM((n_dp, 1, 128), f32),
+            pltpu.VMEM((1, 128), f32),
             pltpu.VMEM((8, 128), jnp.int32),
             pltpu.SMEM((8, 128), jnp.int32),
             pltpu.SemaphoreType.DMA((5,)),
-            pltpu.SemaphoreType.DMA((8,)),
-            pltpu.SemaphoreType.DMA((8,)),
+            pltpu.SemaphoreType.DMA((9,)),
+            pltpu.SemaphoreType.DMA((9,)),
         ],
         compiler_params=pltpu.CompilerParams(
             collective_id=0, has_side_effects=True, vmem_limit_bytes=48 << 20
         ),
         name="soap_step",
-    )(owners, gradient, momentum, eig_left, eig_right, row_stats, col_stats)
+    )(*map(in_hbm, arguments))
+    return pl.pallas_call(
+        store,
+        out_shape=shapes,
+        in_specs=[anywhere] * 4,
+        out_specs=(hbm,) * 4,
+        scratch_shapes=[pltpu.SemaphoreType.DMA((4,))],
+        compiler_params=pltpu.CompilerParams(vmem_limit_bytes=48 << 20),
+        name="store",
+    )(*results)
 
 
 def solution(mesh):

time: 104 us -> 93 us (0.89)
  the two profiles are of different devices: /device:TPU:2 before, /device:TPU:22 now
where the time goes in v2:
time: 93 us; the launch traced here: 92.9 us
  Pallas kernels  92.2 us (99%)
    pallas_call x1, Pallas kernels, local(): pl.pallas_call(functools.partial(kernel, n_dp, n_tensor, clip_norm), out_...  91.2 us

profile of v2, /device:TPU:22, one launch (start us, length us, event | category | flops | bytes accessed | tf_op | source)
XLA Modules:
  0.0 92.9 jit_solution(16095224389193471723)
XLA Ops:
  0.6 91.2 %soap_step.1 = (f32[24,16,512]{2,1,0:T(8,128)S(1)}, bf16[24,16,512]{2,1,0:T(8,128)(2,1)S(1)}, f32[2,512]{1,0:T(2,128)S(1)}, f32[2,512]{1,0:T(2,128)S(1)}) custom-call(s32[1,24]{1,0:T(1,128)} %bitcast.1, bf16[24,16,512]{2,1,0:T(8,128)(2,1)} %gradient.1, f32[24,16,512]{2,1,0:T(8,128)} %momentum.1, bf16[2,512,512]{2,1,0:T(8,128)(2,1)} %left.1, ...), custom_call_target="tpu_custom_call" | custom-call | tf_op jit(solution)/shard_map/soap_step/pallas_call | solution.py:339
  91.8 1.0 %store.1 = (f32[24,16,512]{2,1,0:T(8,128)}, bf16[24,16,512]{2,1,0:T(8,128)(2,1)}, f32[2,512]{1,0:T(2,128)}, f32[2,512]{1,0:T(2,128)}) custom-call(f32[24,16,512]{2,1,0:T(8,128)S(1)} %get-tuple-element.8.refs_0_, bf16[24,16,512]{2,1,0:T(8,128)(2,1)S(1)} %get-tuple-element.9.refs_1_, f32[2,512]{1,0:T(2,128)S(1)} %get-tuple-element.10.refs_2_, ...), custom_call_target="tpu_custom_call" | custom-call | tf_op jit(solution)/shard_map/store/pallas_call | solution.py:382

commit v3 on v2

--- a/solution.py
+++ b/solution.py
@@ -14,6 +14,7 @@
 clip_share = 0.25
 columns = 8
 lead = 11
+extra = 4
 chunk = 128
 MESH = pl.DeviceIdType.MESH
 f32 = jnp.float32
@@ -47,6 +48,7 @@
     update,
     new_rows,
     new_cols,
+    flags,
     grad_v,
     mom_v,
     moment_v,
@@ -62,6 +64,10 @@
     in_g,
     in_m,
     in_u,
+    ring_g,
+    ring_m,
+    band_g,
+    band_m,
     sums_t,
     sums_d,
     total,
@@ -70,10 +76,13 @@
     local_sem,
     send_sem,
     recv_sem,
+    ring_send_sem,
+    ring_recv_sem,
 ):
     blocks, strip, size = grad_v.shape
     me = lax.axis_index("tensor")
     group = lax.axis_index("dp")
+    rows = n_tensor // columns
     my_x = me // columns
     my_y = lax.rem(me, columns)
     barrier = pltpu.get_barrier_semaphore()
@@ -109,7 +118,23 @@
         mine = lane == owners[0, b]
         second = jnp.where(mine & (first >= 0), b, second)
         first = jnp.where(mine & (first < 0), b, first)
-    chosen_v[...] = jnp.where(level == 0, first, second)
+    double = (second >= 0).astype(jnp.int32)
+    number = double
+    for shift in (1, 2, 4, 8, 16):
+        number = number + jnp.where(lane >= shift, pltpu.roll(number, shift, 1), 0)
+    number = number - double
+    listed = jnp.zeros((8, 128), jnp.int32)
+    for j in range(extra):
+        found = jnp.where((double > 0) & (number == j), second, 0)
+        listed = jnp.where(lane == j, jnp.sum(found, axis=1, keepdims=True), listed)
+    crowded = jnp.sum(double, axis=1, keepdims=True) > extra
+    chosen_v[...] = jnp.where(
+        level == 0,
+        first,
+        jnp.where(
+            level == 1, second, jnp.where(level == 2, listed, jnp.minimum(number, extra - 1))
+        ),
+    )
     load_c = pltpu.make_async_copy(chosen_v, chosen, local_sem.at[4])
     load_c.start()
     load_g.wait()
@@ -122,33 +147,100 @@
                 total = total + wide[8 * i : 8 * i + 8, 128 * j : 128 * j + 128]
         return total
 
-    mine = lax.fori_loop(0, blocks, squares, jnp.zeros((8, 128), f32))
-    sums_t[me] = jnp.sum(mine, axis=0, keepdims=True)
-
-    def pack(source, target, k):
-        @pl.loop(0, n_tensor, unroll=4)
-        def _(p):
-            target[k, p] = source[jnp.maximum(chosen[k, p], 0)]
+    part = lax.fori_loop(0, blocks, squares, jnp.zeros((8, 128), f32))
+    part = jnp.sum(part + pltpu.roll(part, 64, 1), axis=0, keepdims=True)
+    sums_t[me] = jnp.where(lane[0:1] < 64, part, crowded[0:1].astype(f32))
 
     def strip_of(p):
         return pl.ds(pl.multiple_of(p * strip, strip), strip)
 
-    def scatter(source, target, k, number):
-        @pl.loop(1, n_tensor)
-        def _(i):
-            dx = i // columns
-            j = lax.rem(i, columns)
-            odd = lax.rem(j, 2)
-            dy = odd * ((j + 1) // 2) + (1 - odd) * lax.rem(columns - j // 2, columns)
-            p = lax.rem(my_x + dx, n_tensor // columns) * columns + lax.rem(my_y + dy, columns)
+    def band_of(c):
+        return pl.ds(pl.multiple_of(c * chunk, chunk), chunk)
+
+    def turned(i):
+        return lax.rem(my_y + i + columns, columns)
+
+    def exchange(source, outgoing, ring, band, target, phase, meanwhile):
+        def start(src, dst, send, recv, peer):
             pltpu.make_async_remote_copy(
-                src_ref=source.at[k, p],
-                dst_ref=target.at[k, strip_of(me)],
-                send_sem=send_sem.at[number],
-                recv_sem=recv_sem.at[number],
-                device_id={"tensor": p},
+                src_ref=src,
+                dst_ref=dst,
+                send_sem=send,
+                recv_sem=recv,
+                device_id={"tensor": peer},
                 device_id_type=MESH,
             ).start()
+
+        def shares(hop):
+            whole = pl.ds(0, extra)
+            low, high = pl.ds(0, extra // 2), pl.ds(extra // 2, extra // 2)
+            return (whole, whole) if hop < columns // 2 else (low, high)
+
+        def pass_on(hop):
+            for way, share in zip((1, -1), shares(hop)):
+                entry = ring.at[turned(-way * (hop - 1)), share]
+                start(
+                    entry,
+                    entry,
+                    ring_send_sem.at[phase],
+                    ring_recv_sem.at[phase, 2 * hop - 2 + (way < 0)],
+                    my_x * columns + turned(way),
+                )
+
+        def arrive(hop):
+            for way, share in zip((1, -1), shares(hop)):
+                entry = ring.at[turned(-way * hop), share]
+                pltpu.make_async_remote_copy(
+                    src_ref=entry,
+                    dst_ref=entry,
+                    send_sem=ring_send_sem.at[phase],
+                    recv_sem=ring_recv_sem.at[phase, 2 * hop - 2 + (way < 0)],
+                    device_id={"tensor": my_x * columns + turned(way)},
+                    device_id_type=MESH,
+                ).wait_recv()
+
+        def scatter(dx):
+            row = lax.rem(my_x + dx, rows) * columns
+
+            @pl.loop(1 if dx == 0 else 0, columns)
+            def _(i):
+                odd = lax.rem(i, 2)
+                p = row + turned(odd * ((i + 1) // 2) - (1 - odd) * (i // 2))
+                outgoing[p] = source[jnp.maximum(chosen[0, p], 0)]
+                start(
+                    outgoing.at[p],
+                    target.at[0, strip_of(me)],
+                    send_sem.at[2 + 2 * phase],
+                    recv_sem.at[2 + 2 * phase],
+                    p,
+                )
+
+        for j in range(extra):
+            ring[my_y, j] = source[chosen[2, j]]
+        pass_on(1)
+        target[0, strip_of(me)] = source[jnp.maximum(chosen[0, me], 0)]
+        scatter(0)
+        for hop in range(1, columns // 2):
+            scatter(hop)
+            arrive(hop)
+            pass_on(hop + 1)
+            if hop in meanwhile:
+                meanwhile[hop]()
+        arrive(columns // 2)
+        for c in range(rows):
+            j = chosen[3, c * columns + my_y]
+            for y in range(columns):
+                band[c, strip * y : strip * (y + 1)] = ring[y, j]
+        target[1, band_of(my_x)] = band[my_x]
+        for i in range(1, rows):
+            c = lax.rem(my_x + i, rows)
+            start(
+                band.at[c],
+                target.at[1, band_of(my_x)],
+                send_sem.at[3 + 2 * phase],
+                recv_sem.at[3 + 2 * phase],
+                c * columns + my_y,
+            )
 
     def waiter(ref, number):
         return pltpu.make_async_remote_copy(
@@ -160,7 +252,7 @@
             device_id_type=MESH,
         )
 
-    others = pl.ds(0, (n_tensor - 1) * strip)
+    others = (pl.ds(0, (n_tensor - 1) * strip), pl.ds(0, (rows - 1) * chunk))
 
     def send_sum(source, target, number, peer):
         pltpu.make_async_remote_copy(
@@ -186,35 +278,38 @@
             peer = {"dp": lax.rem(group + i, n_dp)}
             send_sum(sums_d.at[group], sums_d.at[group], 1, peer)
 
-        waiter(sum_of_d, 1).wait_recv()
-        total[...] = jnp.sum(sums_d[...], axis=0)
-
-        @pl.loop(1, n_tensor)
-        def _(i):
-            send_sum(total, total, 8, {"tensor": lax.rem(lead + i, n_tensor)})
-
     @pl.when(me != lead)
     def _():
         pl.semaphore_wait(barrier, n_tensor - 1)
         send_sum(sums_t.at[me], sums_t.at[me], 0, {"tensor": lead})
 
     load_c.wait()
-    for k in range(2):
-        pack(grad_v, out_g, k)
-        scatter(out_g, in_g, k, 2 + k)
-        in_g[k, strip_of(me)] = out_g[k, me]
-    load_l.wait()
-    load_r.wait()
-    for k in range(2):
-        left_t[k] = left_v[k].T
-        right_t[k] = right_v[k].T
+    def announce():
+        @pl.when(me == lead)
+        def _():
+            waiter(sum_of_d, 1).wait_recv()
+            total[...] = jnp.sum(sums_d[...], axis=0)
+
+            @pl.loop(1, n_tensor)
+            def _(i):
+                send_sum(total, total, 8, {"tensor": lax.rem(lead + i, n_tensor)})
+
+    def transpose():
+        load_l.wait()
+        load_r.wait()
+        for k in range(2):
+            left_t[k] = left_v[k].T
+            right_t[k] = right_v[k].T
+
+    exchange(grad_v, out_g, ring_g, band_g, in_g, 0, {2: announce, 3: transpose})
     load_m.wait()
 
     @pl.when(me != lead)
     def _():
         waiter(total, 8).wait_recv()
 
-    squared_sum = jnp.sum(total[...], keepdims=True)
+    flags[...] = total[...]
+    squared_sum = jnp.sum(jnp.where(lane[0:1] < 64, total[...], 0.0), keepdims=True)
     limit = clip_norm * clip_norm
     factor = jnp.where(
         squared_sum > limit, clip_norm / jnp.sqrt(jnp.maximum(squared_sum, limit)), 1.0
@@ -229,14 +324,9 @@
 
     store_m = pltpu.make_async_copy(mom_v, new_momentum, local_sem.at[1])
     store_m.start()
-    for k in range(2):
-        pack(moment_v, out_m, k)
-        scatter(out_m, in_m, k, 4 + k)
-        in_m[k, strip_of(me)] = out_m[k, me]
-
     share = factor * factor * ((1.0 - second_decay) / size)
-    for k in range(2):
-        waiter(in_g.at[k, others], 2 + k).wait_recv()
+    def statistics(k):
+        waiter(in_g.at[k, others[k]], 2 + k).wait_recv()
         half = dot(left_t[k], in_g[k]).astype(bf16)
         rotated = dot(half, right_v[k])
         square = rotated * rotated
@@ -252,13 +342,24 @@
         new_rows[k : k + 1, :] = jnp.where(used, to_row(rows_next), rows_old)
         new_cols[k : k + 1, :] = jnp.where(used, cols_next, cols_old)
 
+    exchange(
+        moment_v,
+        out_m,
+        ring_m,
+        band_m,
+        in_m,
+        1,
+        {1: lambda: statistics(0), 3: lambda: statistics(1)},
+    )
+
+
     for k in range(2):
-        waiter(in_m.at[k, others], 4 + k).wait_recv()
+        waiter(in_m.at[k, others[k]], 4 + k).wait_recv()
         half = dot(left_t[k], in_m[k]).astype(bf16)
         direction = (dot(half, right_v[k]) * inverse[k]).astype(bf16)
         for j in range(n_tensor // columns):
             c = lax.rem(my_x + j, n_tensor // columns)
-            band = pl.ds(pl.multiple_of(c * chunk, chunk), chunk)
+            band = band_of(c)
             half_back = dot(left_v[k, band], direction).astype(bf16)
             out_u[k, band] = dot(half_back, right_t[k]).astype(bf16)
 
@@ -298,9 +399,19 @@
         waiter(total, 0).wait_send()
 
     for k in range(2):
-        waiter(in_g.at[k, others], 2 + k).wait_send()
-        waiter(in_m.at[k, others], 4 + k).wait_send()
+        waiter(in_g.at[k, others[k]], 2 + k).wait_send()
+        waiter(in_m.at[k, others[k]], 4 + k).wait_send()
         waiter(in_u.at[k, pl.ds(0, n_tensor - 1)], 6 + k).wait_send()
+    for ring, phase in ((ring_g, 0), (ring_m, 1)):
+        sent = ring.at[pl.ds(0, columns - 1)]
+        pltpu.make_async_remote_copy(
+            src_ref=sent,
+            dst_ref=sent,
+            send_sem=ring_send_sem.at[phase],
+            recv_sem=ring_recv_sem.at[phase, 0],
+            device_id={"tensor": lax.rem(me + 1, n_tensor)},
+            device_id_type=MESH,
+        ).wait_send()
     store_m.wait()
     store_u.wait()
 
@@ -315,6 +426,79 @@
         copy.wait()
 
 
+def precondition(arrived, left_basis, right_basis, row_stats, col_stats, in_use):
+    halves = jnp.einsum(
+        "kij,kcil->kcjl", left_basis, arrived, preferred_element_type=jnp.float32
+    ).astype(jnp.bfloat16)
+    rotated = jnp.einsum("kcjl,klm->kcjm", halves, right_basis, preferred_element_type=jnp.float32)
+    rot_grad = rotated[:, 0]
+    rot_moment = rotated[:, 1]
+    squares = rot_grad * rot_grad
+    rows_next = second_decay * row_stats + (1.0 - second_decay) * jnp.mean(squares, axis=2)
+    cols_next = second_decay * col_stats + (1.0 - second_decay) * jnp.mean(squares, axis=1)
+    scale_hat = (
+        rows_next[:, :, None] * cols_next[:, None, :] / jnp.mean(rows_next, axis=1)[:, None, None]
+    )
+    direction = (rot_moment / (jnp.sqrt(scale_hat) + epsilon)).astype(jnp.bfloat16)
+    half_back = jnp.einsum(
+        "kij,kjl->kil", left_basis, direction, preferred_element_type=jnp.float32
+    ).astype(jnp.bfloat16)
+    finished = jnp.einsum(
+        "kil,kml->kim", half_back, right_basis, preferred_element_type=jnp.float32
+    ).astype(jnp.bfloat16)
+    kept_rows = jnp.where(in_use[:, None], rows_next, row_stats)
+    kept_cols = jnp.where(in_use[:, None], cols_next, col_stats)
+    return (finished, kept_rows, kept_cols)
+
+
+def general(gradient, momentum, eig_left, eig_right, row_stats, col_stats, owners):
+    group_blocks, strip_rows, block_size = gradient.shape
+    owner_slots = eig_left.shape[0]
+    tensor_size = lax.axis_size("tensor")
+    whole_blocks = group_blocks * lax.axis_size("dp")
+    widened = gradient.astype(jnp.float32)
+    squared_sum = lax.psum(jnp.sum(widened * widened), ("dp", "tensor"))
+    factor = jnp.minimum(
+        1.0, clip_share * block_size * math.sqrt(whole_blocks) / jnp.sqrt(squared_sum)
+    )
+    clipped = widened * factor
+    new_momentum = momentum_decay * momentum + (1.0 - momentum_decay) * clipped
+    payload = jnp.stack([clipped.astype(jnp.bfloat16), new_momentum.astype(jnp.bfloat16)], axis=1)
+    payload = payload.reshape(group_blocks, 2, strip_rows * block_size)
+    holders = owners[:, 0]
+    counter = jnp.arange(group_blocks, dtype=jnp.int32)
+    same_owner = holders[:, None] == holders[None, :]
+    before = counter[None, :] < counter[:, None]
+    earlier_count = jnp.sum((same_owner & before).astype(jnp.int32), axis=1)
+    slot_match = (
+        earlier_count[None, None, :] == jnp.arange(owner_slots, dtype=jnp.int32)[:, None, None]
+    )
+    owner_match = holders[None, None, :] == jnp.arange(tensor_size, dtype=jnp.int32)[None, :, None]
+    selector = (slot_match & owner_match).astype(jnp.bfloat16)
+    outgoing = jnp.einsum(
+        "kpb,bcx->kcpx", selector, payload, preferred_element_type=jnp.float32
+    ).astype(jnp.bfloat16)
+    owned_count = jnp.sum((holders == lax.axis_index("tensor")).astype(jnp.int32))
+    in_use = jnp.arange(owner_slots, dtype=jnp.int32) < owned_count
+    arrived = lax.all_to_all(outgoing, "tensor", split_axis=2, concat_axis=2, tiled=True)
+    arrived = arrived.reshape(owner_slots, 2, block_size, block_size)
+    finished, new_rows, new_cols = precondition(
+        arrived, eig_left, eig_right, row_stats, col_stats, in_use
+    )
+    returned = lax.all_to_all(
+        finished.reshape(owner_slots, tensor_size, strip_rows * block_size),
+        "tensor",
+        split_axis=1,
+        concat_axis=1,
+        tiled=True,
+    )
+    update = jnp.einsum(
+        "kpb,kpx->bx", selector, returned, preferred_element_type=jnp.float32
+    ).astype(jnp.bfloat16)
+    update = update.reshape(group_blocks, strip_rows, block_size)
+    return (new_momentum, update, new_rows, new_cols)
+
+
 def in_hbm(x):
     return pltpu.with_memory_space_constraint(x, pltpu.HBM)
 
@@ -327,7 +511,9 @@
     hbm = pl.BlockSpec(memory_space=pltpu.HBM)
     vmem = pl.BlockSpec(memory_space=pltpu.VMEM)
     square = (slots, size, size)
-    pieces = (slots, n_tensor, strip, size)
+    pieces = (n_tensor, strip, size)
+    ring = (columns, extra, strip, size)
+    bands = (n_tensor // columns, chunk, size)
     shapes = (
         jax.ShapeDtypeStruct(momentum.shape, f32),
         jax.ShapeDtypeStruct(gradient.shape, bf16),
@@ -336,9 +522,9 @@
     )
     arguments = (owners.reshape(1, blocks), gradient, momentum)
     arguments += (eig_left, eig_right, row_stats, col_stats)
-    results = pl.pallas_call(
+    *results, flags = pl.pallas_call(
         functools.partial(kernel, n_dp, n_tensor, clip_norm),
-        out_shape=shapes,
+        out_shape=(*shapes, jax.ShapeDtypeStruct((1, 128), f32)),
         in_specs=[
             pl.BlockSpec(memory_space=pltpu.SMEM),
             hbm,
@@ -348,7 +534,7 @@
             vmem,
             vmem,
         ],
-        out_specs=(anywhere, anywhere, vmem, vmem),
+        out_specs=(anywhere, anywhere, vmem, vmem, vmem),
         scratch_shapes=[
             pltpu.VMEM(gradient.shape, bf16),
             pltpu.VMEM(gradient.shape, f32),
@@ -364,7 +550,11 @@
             pltpu.VMEM(square, bf16),
             pltpu.VMEM(square, bf16),
             pltpu.VMEM(square, bf16),
-            pltpu.VMEM(pieces, bf16),
+            pltpu.VMEM((slots, *pieces), bf16),
+            pltpu.VMEM(ring, bf16),
+            pltpu.VMEM(ring, bf16),
+            pltpu.VMEM(bands, bf16),
+            pltpu.VMEM(bands, bf16),
             pltpu.VMEM((n_tensor, 1, 128), f32),
             pltpu.VMEM((n_dp, 1, 128), f32),
             pltpu.VMEM((1, 128), f32),
@@ -373,13 +563,15 @@
             pltpu.SemaphoreType.DMA((5,)),
             pltpu.SemaphoreType.DMA((9,)),
             pltpu.SemaphoreType.DMA((9,)),
+            pltpu.SemaphoreType.DMA((2,)),
+            pltpu.SemaphoreType.DMA((2, columns)),
         ],
         compiler_params=pltpu.CompilerParams(
             collective_id=0, has_side_effects=True, vmem_limit_bytes=48 << 20
         ),
         name="soap_step",
     )(*map(in_hbm, arguments))
-    return pl.pallas_call(
+    keep = pl.pallas_call(
         store,
         out_shape=shapes,
         in_specs=[anywhere] * 4,
@@ -387,7 +579,15 @@
         scratch_shapes=[pltpu.SemaphoreType.DMA((4,))],
         compiler_params=pltpu.CompilerParams(vmem_limit_bytes=48 << 20),
         name="store",
-    )(*results)
+    )
+    inputs = (gradient, momentum, eig_left, eig_right, row_stats, col_stats, owners)
+    return lax.cond(
+        flags[0, 127] > 0.5,
+        lambda done, given: tuple(general(*given)),
+        lambda done, given: tuple(keep(*done)),
+        tuple(results),
+        inputs,
+    )
 
 
 def solution(mesh):

time: 93 us -> 84.6 us (0.910)
  the two profiles are of different devices: /device:TPU:22 before, /device:TPU:64 now
where the time goes in v3:
time: 84.6 us; the launch traced here: 84.4 us
  Pallas kernels  81.4 us (96%)
  between operations  1.41 us (2%)
  local copies, waits for them, and re-layouts  1.35 us (2%)
    pallas_call x1, Pallas kernels, local(): pl.pallas_call(functools.partial(kernel, n_dp, n_tensor, clip_norm), out_...  80.5 us

profile of v3, /device:TPU:64, one launch (start us, length us, event | category | flops | bytes accessed | tf_op | source)
XLA Modules:
  0.0 84.4 jit_solution(17346675148704146923)
XLA Ops:
  0.6 0.0 copy-start.6
  0.6 0.0 copy-start
  0.7 0.0 copy-start.1
  0.7 0.0 copy-start.2
  0.7 0.0 copy-start.4
  0.7 0.0 copy-start.5
  0.7 80.5 %soap_step.1 = (f32[24,16,512]{2,1,0:T(8,128)S(1)}, bf16[24,16,512]{2,1,0:T(8,128)(2,1)S(1)}, f32[2,512]{1,0:T(2,128)S(1)}, f32[2,512]{1,0:T(2,128)S(1)}, f32[1,128]{1,0:T(1,128)S(1)}) custom-call(s32[1,24]{1,0:T(1,128)} %bitcast.48, bf16[24,16,512]{2,1,0:T(8,128)(2,1)} %gradient.1, f32[24,16,512]{2,1,0:T(8,128)} %momentum.1, bf16[2,512,512]{2,1,0:T(8,128)(2,1)} %left.1, ...), custom_call_target="tpu_custom_call" | custom-call | tf_op jit(solution)/shard_map/soap_step/pallas_call | solution.py:525
  81.2 0.6 slice.9
  82.5 0.0 copy-done.6
  82.5 0.0 copy-done
  82.5 0.0 copy-done.1
  82.5 0.0 copy-done.2
  82.5 0.0 copy-done.4
  82.5 0.0 copy-done.5
  82.5 1.2 %conditional.1 = ((f32[24,16,512]{2,1,0:T(8,128)}, bf16[24,16,512]{2,1,0:T(8,128)(2,1)S(1)}, f32[2,512]{1,0:T(2,128)}, f32[2,512]{1,0:T(2,128)})) conditional(s32[]{:T(128)} %bitcast.13, (f32[24,16,512]{2,1,0:T(8,128)S(1)}, bf16[24,16,512]{2,1,0:T(8,128)(2,1)S(1)}, f32[2,512]{1,0:T(2,128)S(1)}, f32[2,512]{1,0:T(2,128)S(1)}) %tuple.14, ...), branch_computations={%region_0.0_spmd, %region_1.9_spmd} | conditional | flops 3307812352 | bytes 54976388 | solution.py:584
  82.5 0.9 %store.1 = (f32[24,16,512]{2,1,0:T(8,128)}, bf16[24,16,512]{2,1,0:T(8,128)(2,1)S(1)}, f32[2,512]{1,0:T(2,128)}, f32[2,512]{1,0:T(2,128)}) custom-call(f32[24,16,512]{2,1,0:T(8,128)S(1)} %get-tuple-element.22.refs_0_, bf16[24,16,512]{2,1,0:T(8,128)(2,1)S(1)} %get-tuple-element.23.refs_1_, f32[2,512]{1,0:T(2,128)S(1)} %get-tuple-element.24.refs_2_, ...), custom_call_target="tpu_custom_call" | custom-call | tf_op jit(solution)/shard_map/cond/branch_0_fun/store/pallas_call | solution.py:587
  83.7 0.0 copy-start.9
  83.7 0.7 copy-done.9
Async XLA Ops:
  0.6 81.8 %copy-start.6 = (s32[24,1]{0,1:T(1,128)S(1)}, s32[24,1]{0,1:T(1,128)}, u32[]{:S(2)}) copy-start(s32[24,1]{0,1:T(1,128)} %param.15) | copy-start | bytes 292
  0.6 81.8 %copy-start = (bf16[24,16,512]{2,1,0:T(8,128)(2,1)S(1)}, bf16[24,16,512]{2,1,0:T(8,128)(2,1)}, u32[]{:S(2)}) copy-start(bf16[24,16,512]{2,1,0:T(8,128)(2,1)} %gradient.1) | copy-start | bytes 1179652
  0.7 81.8 %copy-start.1 = (f32[24,16,512]{2,1,0:T(8,128)S(1)}, f32[24,16,512]{2,1,0:T(8,128)}, u32[]{:S(2)}) copy-start(f32[24,16,512]{2,1,0:T(8,128)} %momentum.1) | copy-start | bytes 2359300
  0.7 81.8 %copy-start.2 = (bf16[2,512,512]{2,1,0:T(8,128)(2,1)S(1)}, bf16[2,512,512]{2,1,0:T(8,128)(2,1)}, u32[]{:S(2)}) copy-start(bf16[2,512,512]{2,1,0:T(8,128)(2,1)} %left.1) | copy-start | bytes 3145732
  0.7 81.8 %copy-start.4 = (f32[2,512]{1,0:T(2,128)S(1)}, f32[2,512]{1,0:T(2,128)}, u32[]{:S(2)}) copy-start(f32[2,512]{1,0:T(2,128)} %row_stats.1) | copy-start | bytes 12292
  0.7 81.8 %copy-start.5 = (f32[2,512]{1,0:T(2,128)S(1)}, f32[2,512]{1,0:T(2,128)}, u32[]{:S(2)}) copy-start(f32[2,512]{1,0:T(2,128)} %col_stats.1) | copy-start | bytes 12292
  83.7 0.7 copy-start.9

commit v4 on v3

--- a/solution.py
+++ b/solution.py
@@ -581,13 +581,14 @@
         name="store",
     )
     inputs = (gradient, momentum, eig_left, eig_right, row_stats, col_stats, owners)
-    return lax.cond(
+    results = lax.cond(
         flags[0, 127] > 0.5,
         lambda done, given: tuple(general(*given)),
-        lambda done, given: tuple(keep(*done)),
+        lambda done, given: done,
         tuple(results),
         inputs,
     )
+    return keep(*results)
 
 
 def solution(mesh):

time: 84.6 us -> 84.1 us (level)
  no operation moved by 1% of the time
where the time goes in v4:
time: 84.1 us; the launch traced here: 84 us
  Pallas kernels  81.6 us (97%)
  between operations  1.58 us (2%)
    pallas_call x1, Pallas kernels, local(): pl.pallas_call(functools.partial(kernel, n_dp, n_tensor, clip_norm), out_...  80.5 us

profile of v4, /device:TPU:64, one launch (start us, length us, event | category | flops | bytes accessed | tf_op | source)
XLA Modules:
  0.0 84.0 jit_solution(9018909877984943503)
XLA Ops:
  0.6 0.0 copy-start.7
  0.6 0.0 copy-start
  0.7 0.0 copy-start.1
  0.7 0.0 copy-start.2
  0.7 0.0 copy-start.5
  0.7 0.0 copy-start.6
  0.7 80.5 %soap_step.1 = (f32[24,16,512]{2,1,0:T(8,128)S(1)}, bf16[24,16,512]{2,1,0:T(8,128)(2,1)S(1)}, f32[2,512]{1,0:T(2,128)S(1)}, f32[2,512]{1,0:T(2,128)S(1)}, f32[1,128]{1,0:T(1,128)S(1)}) custom-call(s32[1,24]{1,0:T(1,128)} %bitcast.49, bf16[24,16,512]{2,1,0:T(8,128)(2,1)} %gradient.1, f32[24,16,512]{2,1,0:T(8,128)} %momentum.1, bf16[2,512,512]{2,1,0:T(8,128)(2,1)} %left.1, ...), custom_call_target="tpu_custom_call" | custom-call | tf_op jit(solution)/shard_map/soap_step/pallas_call | solution.py:525
  81.2 0.6 slice.9
  82.5 0.0 copy-done.7
  82.5 0.0 copy-done
  82.5 0.0 copy-done.1
  82.5 0.0 copy-done.2
  82.5 0.0 copy-done.5
  82.5 0.0 copy-done.6
  82.5 0.2 conditional.1
  82.8 1.0 %store.1 = (f32[24,16,512]{2,1,0:T(8,128)}, bf16[24,16,512]{2,1,0:T(8,128)(2,1)}, f32[2,512]{1,0:T(2,128)}, f32[2,512]{1,0:T(2,128)}) custom-call(f32[24,16,512]{2,1,0:T(8,128)S(1)} %get-tuple-element.47.refs_0_, bf16[24,16,512]{2,1,0:T(8,128)(2,1)S(1)} %get-tuple-element.48.refs_1_, f32[2,512]{1,0:T(2,128)S(1)} %get-tuple-element.49.refs_2_, ...), custom_call_target="tpu_custom_call" | custom-call | tf_op jit(solution)/shard_map/store/pallas_call | solution.py:591
Async XLA Ops:
  0.6 81.8 %copy-start.7 = (s32[24,1]{0,1:T(1,128)S(1)}, s32[24,1]{0,1:T(1,128)}, u32[]{:S(2)}) copy-start(s32[24,1]{0,1:T(1,128)} %param.15) | copy-start | bytes 292
  0.6 81.8 %copy-start = (bf16[24,16,512]{2,1,0:T(8,128)(2,1)S(1)}, bf16[24,16,512]{2,1,0:T(8,128)(2,1)}, u32[]{:S(2)}) copy-start(bf16[24,16,512]{2,1,0:T(8,128)(2,1)} %gradient.1) | copy-start | bytes 1179652
  0.7 81.8 %copy-start.1 = (f32[24,16,512]{2,1,0:T(8,128)S(1)}, f32[24,16,512]{2,1,0:T(8,128)}, u32[]{:S(2)}) copy-start(f32[24,16,512]{2,1,0:T(8,128)} %momentum.1) | copy-start | bytes 2359300
  0.7 81.8 %copy-start.2 = (bf16[2,512,512]{2,1,0:T(8,128)(2,1)S(1)}, bf16[2,512,512]{2,1,0:T(8,128)(2,1)}, u32[]{:S(2)}) copy-start(bf16[2,512,512]{2,1,0:T(8,128)(2,1)} %left.1) | copy-start | bytes 3145732
  0.7 81.8 %copy-start.5 = (f32[2,512]{1,0:T(2,128)S(1)}, f32[2,512]{1,0:T(2,128)}, u32[]{:S(2)}) copy-start(f32[2,512]{1,0:T(2,128)} %row_stats.1) | copy-start | bytes 12292
  0.7 81.8 %copy-start.6 = (f32[2,512]{1,0:T(2,128)S(1)}, f32[2,512]{1,0:T(2,128)}, u32[]{:S(2)}) copy-start(f32[2,512]{1,0:T(2,128)} %col_stats.1) | copy-start | bytes 12292
